TPU v7x, 32 devices: a whole 2x2x4 slice. The times are simulated.
32 devices in a mesh: mode: 4 (over z), rows: 8 (over y, x, core).
Axes of the slice: x: 2, y: 2, z: 4, core: 2. Of those that a mesh axis runs over, the one named last changes fastest.
Arguments:
- object_real: float32 [8, 2048, 2048], P('mode', 'rows'), may hold values from -6 to 6
- object_imag: float32 [8, 2048, 2048], P('mode', 'rows'), may hold values from -6 to 6
- pupil_real: float32 [1024, 1024], P('rows'), may hold values from -0.7 to 0.7
- pupil_imag: float32 [1024, 1024], P('rows'), may hold values from -0.7 to 0.7
- measured: float32 [1, 1024, 1024], P(None, 'rows'), may hold values from 1 to 5
- source_mask: int32 [1, 3], replicated, may hold values from 0 to 1, as said below
- offsets: int32 [3, 2], replicated, may hold values from 0 to 1024
Outputs:
- updated_real: float32 [8, 2048, 2048], P('mode', 'rows')
- updated_imag: float32 [8, 2048, 2048], P('mode', 'rows')
Inputs may be any that keep to these rules, and one draw needn't show every extreme that they name: `source_mask`: every frame has at least one LED lit and at least one dark.
All inputs are finite; a program needn't handle non-finite values.
Results may differ from a plain program's by a relative error of at most 0.0003.
Values sent between devices are 32-bit elements; how exact they have to be, the bound alone decides.
No kernel may reach another device: no remote copies, remote signals or barrier semaphores. Data moves between devices by JAX's collectives and lax.ppermute only.
A program may use at most 128 MiB of HBM per device.

v0:
```python
import math

import jax
import jax.numpy as jnp
from jax import lax
from jax.sharding import PartitionSpec as P

FLOOR_TERM = 0.5
HIGHEST_PREC = lax.Precision.HIGHEST


def dft_tables(length):
    indices = jnp.arange(length, dtype=jnp.int32)
    phases = indices[:, None] * indices[None, :] % length
    angles = phases.astype(jnp.float32) * (2.0 * math.pi / length)
    scale_factor = 1.0 / math.sqrt(length)
    cos_table = jnp.cos(angles) * scale_factor
    sin_table = jnp.sin(angles) * scale_factor
    return (
        jnp.concatenate([cos_table, sin_table], axis=1),
        jnp.concatenate([cos_table, sin_table], axis=0),
    )


def transform(form, table, real_part, imag_part, axis, direction_sign):
    result = jnp.einsum(form, jnp.stack([real_part, imag_part]), table, precision=HIGHEST_PREC)
    length = result.shape[axis] // 2
    with_cos = lax.slice_in_dim(result, 0, length, axis=axis)
    with_sin = lax.slice_in_dim(result, length, 2 * length, axis=axis)
    return (with_cos[0] - direction_sign * with_sin[1], with_cos[1] + direction_sign * with_sin[0])


def right_product(real_part, imag_part, wide_cols, direction_sign):
    return transform("smlck,kj->smlcj", wide_cols, real_part, imag_part, 4, direction_sign)


def forward_fields(
    part_real, part_imag, pupil_real, pupil_imag, offsets, wide_cols, wide_rows, length
):
    source_count = offsets.shape[0]
    groups = lax.axis_size("rows")
    crop_real = jnp.stack(
        [
            lax.dynamic_slice_in_dim(part_real, offsets[source_index, 1], length, 2)
            for source_index in range(source_count)
        ],
        axis=1,
    )
    crop_imag = jnp.stack(
        [
            lax.dynamic_slice_in_dim(part_imag, offsets[source_index, 1], length, 2)
            for source_index in range(source_count)
        ],
        axis=1,
    )
    got_real, got_imag = (
        lax.all_to_all(
            jnp.swapaxes(crop_real, 2, 3), "rows", split_axis=2, concat_axis=3, tiled=True
        ),
        lax.all_to_all(
            jnp.swapaxes(crop_imag, 2, 3), "rows", split_axis=2, concat_axis=3, tiled=True
        ),
    )
    win_real = jnp.stack(
        [
            lax.dynamic_slice_in_dim(got_real[:, source_index], offsets[source_index, 0], length, 2)
            for source_index in range(source_count)
        ],
        axis=1,
    )
    win_imag = jnp.stack(
        [
            lax.dynamic_slice_in_dim(got_imag[:, source_index], offsets[source_index, 0], length, 2)
            for source_index in range(source_count)
        ],
        axis=1,
    )
    lifted_real = pupil_real * win_real - pupil_imag * win_imag
    lifted_imag = pupil_real * win_imag + pupil_imag * win_real
    half_real, half_imag = transform("smlcr,yr->smlyc", wide_rows, lifted_real, lifted_imag, 3, 1.0)
    layout = half_real.shape
    blocked = (layout[0], layout[1], groups, layout[2] // groups, layout[3])
    back_real, back_imag = (
        lax.all_to_all(half_real.reshape(blocked), "rows", split_axis=2, concat_axis=4, tiled=True),
        lax.all_to_all(half_imag.reshape(blocked), "rows", split_axis=2, concat_axis=4, tiled=True),
    )
    flat = (layout[0], layout[1], layout[2] // groups, layout[3] * groups)
    return right_product(back_real.reshape(flat), back_imag.reshape(flat), wide_cols, 1.0)


def spectral_updates(diff_real, diff_imag, pupil_real, pupil_imag, offsets, wide_cols, size_k):
    source_count = offsets.shape[0]
    groups = lax.axis_size("rows")
    col_real, col_imag = right_product(diff_real, diff_imag, wide_cols, -1.0)
    layout = col_real.shape
    blocked = (layout[0], layout[1], layout[2], groups, layout[3] // groups)
    got_real, got_imag = (
        lax.all_to_all(col_real.reshape(blocked), "rows", split_axis=3, concat_axis=2, tiled=True),
        lax.all_to_all(col_imag.reshape(blocked), "rows", split_axis=3, concat_axis=2, tiled=True),
    )
    flat = (layout[0], layout[1], layout[2] * groups, layout[3] // groups)
    full_real = got_real.reshape(flat)
    full_imag = got_imag.reshape(flat)
    delta_real, delta_imag = transform("smlyc,yk->smlck", wide_cols, full_real, full_imag, 4, -1.0)
    upd_real = pupil_real * delta_real + pupil_imag * delta_imag
    upd_imag = pupil_real * delta_imag - pupil_imag * delta_real
    blank = jnp.zeros((layout[0], layout[3] // groups, size_k), jnp.float32)
    placed_real = jnp.stack(
        [
            lax.dynamic_update_slice_in_dim(
                blank, upd_real[:, source_index], offsets[source_index, 0], 2
            )
            for source_index in range(source_count)
        ],
        axis=1,
    )
    placed_imag = jnp.stack(
        [
            lax.dynamic_update_slice_in_dim(
                blank, upd_imag[:, source_index], offsets[source_index, 0], 2
            )
            for source_index in range(source_count)
        ],
        axis=1,
    )
    return (
        lax.all_to_all(placed_real, "rows", split_axis=3, concat_axis=2, tiled=True),
        lax.all_to_all(placed_imag, "rows", split_axis=3, concat_axis=2, tiled=True),
    )


def add_window(target, incoming, start_col, length):
    current = lax.dynamic_slice_in_dim(target, start_col, length, 2)
    return lax.dynamic_update_slice_in_dim(
        target, current + jnp.swapaxes(incoming, 1, 2), start_col, 2
    )


def body(object_real, object_imag, pupil_real, pupil_imag, measured, source_mask, offsets):
    length = pupil_real.shape[1]
    size_k = object_real.shape[2]
    source_count = offsets.shape[0]
    wide_cols, wide_rows = dft_tables(length)
    spec_real, spec_imag = (object_real, object_imag)
    weights = source_mask[0].astype(jnp.float32)
    field_real, field_imag = forward_fields(
        spec_real, spec_imag, pupil_real, pupil_imag, offsets, wide_cols, wide_rows, length
    )
    powers = jnp.sum(field_real * field_real + field_imag * field_imag, axis=0)
    partial_sum = jnp.tensordot(weights, powers, axes=1)
    share = lax.psum_scatter(partial_sum, "mode", scatter_dimension=0, tiled=True)
    share_rows = share.shape[0]
    measured_share = lax.dynamic_slice_in_dim(
        measured[0], lax.axis_index("mode") * share_rows, share_rows, 0
    )
    ratio_share = measured_share / jnp.sqrt(share + FLOOR_TERM)
    ratios = lax.all_gather(ratio_share, "mode", axis=0, tiled=True)
    factor = (ratios - 1.0)[None, None] * weights[None, :, None, None]
    diff_real = field_real * factor
    diff_imag = field_imag * factor
    ret_real, ret_imag = spectral_updates(
        diff_real, diff_imag, pupil_real, pupil_imag, offsets, wide_cols, size_k
    )
    for source_index in range(source_count):
        start_col = offsets[source_index, 1]
        spec_real = add_window(spec_real, ret_real[:, source_index], start_col, length)
        spec_imag = add_window(spec_imag, ret_imag[:, source_index], start_col, length)
    return (spec_real, spec_imag)


def solution(mesh):
    in_specs = (
        P("mode", "rows", None),
        P("mode", "rows", None),
        P("rows", None),
        P("rows", None),
        P(None, "rows", None),
        P(),
        P(),
    )
    out_specs = (P("mode", "rows", None), P("mode", "rows", None))
    return jax.shard_map(body, mesh=mesh, in_specs=in_specs, out_specs=out_specs, check_vma=False)
```

profile of v0, /device:TPU:0, one launch (start us, length us, event | category | flops | bytes accessed | tf_op | source)
XLA Modules:
  0.0 903.5 jit_solution(336317563343910032)
XLA Ops:
  35.8 7.3 maximum_bitcast_fusion.3
  56.4 10.3 %copy.142 = f32[2,3,1024,256]{3,0,1,2:T(2,128)} copy(f32[2,3,1024,256]{2,3,0,1:T(8,128)} %maximum_bitcast_fusion.4) | data formatting | bytes 12582912 | tf_op jit(solution)/shard_map/transpose | solution.py:61
  66.7 53.4 %all-to-all-done = f32[2,3,1024,256]{3,0,1,2:T(2,128)} async-done(((f32[2,3,1024,256]{3,0,1,2:T(2,128)}), f32[2,3,1024,256]{3,0,1,2:T(2,128)}, u32[]{:S(2)}, u32[]{:S(2)}) %all-to-all-start) | async-done | bytes 6291488 | tf_op jit(solution)/shard_map/all_to_all | solution.py:57
  130.2 17.8 %sine_multiply_fusion = (f32[1024,1024]{1,0:T(8,128)}, f32[1024,1024]{1,0:T(8,128)}) fusion(), kind=kLoop, calls=%fused_computation.31 | loop fusion | flops 16777216 | bytes 8388608 | tf_op jit(solution)/shard_map/mul | solution.py:18
  168.9 27.8 %all-to-all-done.1 = f32[2,3,1024,256]{3,0,1,2:T(2,128)} async-done(((f32[2,3,1024,256]{3,0,1,2:T(2,128)}), f32[2,3,1024,256]{3,0,1,2:T(2,128)}, u32[]{:S(2)}, u32[]{:S(2)}) %all-to-all-start.1) | async-done | bytes 6291488 | tf_op jit(solution)/shard_map/all_to_all | solution.py:60
  233.3 56.5 %fusion.18 = f32[2,2,3,2048,128]{4,3,2,1,0:T(8,128)S(1)} fusion(f32[1,2,3,128,1024]{4,3,2,1,0:T(8,128)} %get-tuple-element.19, f32[1,2,3,128,1024]{4,3,2,1,0:T(8,128)} %get-tuple-element.18, f32[1024,1024]{1,0:T(8,128)S(1)} %copy-done.7, f32[1024,1024]{1,0:T(8,128)S(1)} %copy-done.8), kind=kOutput, calls=%fused_computation.27 | convolution fusion | flops 38658375680 | bytes 27262976 | tf_op jit(solution)/shard_map/smlcr,yr->smlyc/dot_general | solution.py:26
  298.7 36.0 %all-to-all-done.2 = f32[2,3,8,128,128]{4,3,1,0,2:T(8,128)} async-done(((f32[2,3,8,128,128]{4,3,1,0,2:T(8,128)}), f32[2,3,8,128,128]{4,3,1,0,2:T(8,128)}, u32[]{:S(2)}, u32[]{:S(2)}) %all-to-all-start.2) | async-done | bytes 3145760 | tf_op jit(solution)/shard_map/all_to_all | solution.py:84
  348.4 27.8 %all-to-all-done.3 = f32[2,3,8,128,128]{4,3,1,0,2:T(8,128)S(1)} async-done(((f32[2,3,8,128,128]{4,3,1,0,2:T(8,128)}), f32[2,3,8,128,128]{4,3,1,0,2:T(8,128)S(1)}, u32[]{:S(2)}, u32[]{:S(2)}) %all-to-all-start.3) | async-done | bytes 3145760 | tf_op jit(solution)/shard_map/all_to_all | solution.py:85
  384.4 43.9 %fusion.6 = f32[2,2,3,128,2048]{4,3,2,1,0:T(8,128)S(1)} fusion(f32[1,2,3,128,1024]{4,3,2,1,0:T(8,128)} %stack_reshape.13, f32[1,2,3,128,1024]{4,3,2,1,0:T(8,128)S(1)} %copy-done.12, f32[1024,1024]{1,0:T(8,128)} %get-tuple-element.50, f32[1024,1024]{1,0:T(8,128)} %get-tuple-element.51), kind=kOutput, calls=%fused_computation.10 | convolution fusion | flops 38658375680 | bytes 27262976 | tf_op jit(solution)/shard_map/smlck,kj->smlcj/dot_general | solution.py:26
  434.8 22.0 %reduce-scatter.2.cloned.1.call-done = f32[32,1024]{1,0:T(8,128)} async-done(((f32[128,1024]{1,0:T(8,128)}), f32[32,1024]{1,0:T(8,128)}) %reduce-scatter.2.cloned.1.call-update) | async-done | bytes 131088 | tf_op jit(solution)/shard_map/reduce_scatter | solution.py:151
  457.8 15.8 %all_gather.3 = f32[128,1024]{1,0:T(8,128)S(1)} all-gather(f32[32,1024]{1,0:T(8,128)S(1)} %bitcast_multiply_fusion), channel_id=1, replica_groups=mesh['mode'=4,'rows'=8] {'mode'}, dimensions={0}, use_global_device_ids=true | all-gather | bytes 655360 | tf_op jit(solution)/shard_map/all_gather | solution.py:157
  473.9 8.2 broadcast_multiply_fusion.1
  482.0 46.2 %fusion.10 = f32[2,2,3,128,2048]{4,3,2,1,0:T(8,128)S(1)} fusion(f32[1,2,3,128,1024]{4,3,2,1,0:T(8,128)} %get-tuple-element.11, f32[1,2,3,128,1024]{4,3,2,1,0:T(8,128)S(1)} %get-tuple-element.10, f32[1024,1024]{1,0:T(8,128)} %get-tuple-element.50, f32[1024,1024]{1,0:T(8,128)} %get-tuple-element.51), kind=kOutput, calls=%fused_computation.14 | convolution fusion | flops 38658375680 | bytes 27262976 | tf_op jit(solution)/shard_map/smlck,kj->smlcj/dot_general | solution.py:26
  540.6 34.9 %all-to-all-done.4 = f32[2,3,128,8,128]{4,2,1,0,3:T(8,128)} async-done(((f32[2,3,128,8,128]{4,2,1,0,3:T(8,128)}), f32[2,3,128,8,128]{4,2,1,0,3:T(8,128)}, u32[]{:S(2)}, u32[]{:S(2)}) %all-to-all-start.4) | async-done | bytes 3145760 | tf_op jit(solution)/shard_map/all_to_all | solution.py:98
  587.3 29.7 %all-to-all-done.5 = f32[2,3,128,8,128]{4,2,1,0,3:T(8,128)S(1)} async-done(((f32[2,3,128,8,128]{4,2,1,0,3:T(8,128)}), f32[2,3,128,8,128]{4,2,1,0,3:T(8,128)S(1)}, u32[]{:S(2)}, u32[]{:S(2)}) %all-to-all-start.5) | async-done | bytes 3145760 | tf_op jit(solution)/shard_map/all_to_all | solution.py:99
  624.1 43.6 %fusion.14 = f32[2,2,3,128,2048]{4,3,2,1,0:T(8,128)S(1)} fusion(f32[1,2,3,1024,128]{3,4,2,1,0:T(8,128)} %stack_reshape.15, f32[1,2,3,1024,128]{3,4,2,1,0:T(8,128)S(1)} %copy-done.11, f32[1024,1024]{1,0:T(8,128)} %get-tuple-element.50, f32[1024,1024]{1,0:T(8,128)} %get-tuple-element.51), kind=kOutput, calls=%fused_computation.18 | convolution fusion | flops 38658375680 | bytes 27262976 | tf_op jit(solution)/shard_map/smlyc,yk->smlck/dot_general | solution.py:26
  704.8 58.1 %all-to-all-done.7 = f32[2,3,128,2048]{2,0,1,3:T(2,128)} async-done(((f32[2,3,128,2048]{2,0,1,3:T(2,128)}), f32[2,3,128,2048]{2,0,1,3:T(2,128)}, u32[]{:S(2)}, u32[]{:S(2)}) %all-to-all-start.7) | async-done | bytes 6291488 | tf_op jit(solution)/shard_map/all_to_all | solution.py:128
  802.5 7.0 dynamic_update_slice.51
  820.9 7.0 dynamic_update_slice.53
  839.2 9.1 %copy.159 = f32[2,3,8,128,256]{3,2,4,0,1:T(8,128)} copy(f32[2,3,8,128,256]{3,0,1,4,2:T(2,128)} %bitcast.48) | data formatting | bytes 12582912 | tf_op jit(solution)/shard_map/all_to_all | solution.py:127
  848.3 7.3 all_to_all.119
  858.9 10.8 %dynamic_update_slice.45 = f32[2,256,2048]{2,1,0:T(8,128)} dynamic-update-slice(f32[2,256,2048]{2,1,0:T(8,128)} %copy.195, f32[2,256,1024]{2,1,0:T(8,128)} %fusion.37, s32[]{:T(128)} %constant.41.clone.1, s32[]{:T(128)} %constant.41.clone.1, s32[]{:T(128)S(6)} %select_n.27) | dynamic-update-slice | bytes 4194308 | tf_op jit(solution)/shard_map/dynamic_update_slice | solution.py:134
  872.6 9.5 %dynamic_update_slice.46 = f32[2,256,2048]{2,1,0:T(8,128)} dynamic-update-slice(f32[2,256,2048]{2,1,0:T(8,128)} %dynamic_update_slice.45, f32[2,256,1024]{2,1,0:T(8,128)S(1)} %fusion.36, s32[]{:T(128)} %constant.41.clone.1, s32[]{:T(128)} %constant.41.clone.1, s32[]{:T(128)S(6)} %select_n.29) | dynamic-update-slice | bytes 4194308 | tf_op jit(solution)/shard_map/dynamic_update_slice | solution.py:134
  885.0 11.3 %dynamic_update_slice.47 = f32[2,256,2048]{2,1,0:T(8,128)} dynamic-update-slice(f32[2,256,2048]{2,1,0:T(8,128)} %dynamic_update_slice.46, f32[2,256,1024]{2,1,0:T(8,128)S(1)} %fusion.35, s32[]{:T(128)} %constant.41.clone.1, s32[]{:T(128)} %constant.41.clone.1, s32[]{:T(128)S(6)} %select_n.30) | dynamic-update-slice | bytes 4194308 | tf_op jit(solution)/shard_map/dynamic_update_slice | solution.py:134
  (130 shorter events, 276.7 us)
Async XLA Ops:
  7.2 4.7 copy-start.15
  24.7 6.8 copy-start.1
  31.6 4.3 copy-start.3
  43.1 77.0 %all-to-all-start = ((f32[2,3,1024,256]{3,0,1,2:T(2,128)}), f32[2,3,1024,256]{3,0,1,2:T(2,128)}, u32[]{:S(2)}, u32[]{:S(2)}) async-start(f32[2,3,1024,256]{3,0,1,2:T(2,128)} %maximum_bitcast_fusion.3), calls=%async_computation | async-start | bytes 12582912 | tf_op jit(solution)/shard_map/all_to_all | solution.py:57
  120.1 76.6 %all-to-all-start.1 = ((f32[2,3,1024,256]{3,0,1,2:T(2,128)}), f32[2,3,1024,256]{3,0,1,2:T(2,128)}, u32[]{:S(2)}, u32[]{:S(2)}) async-start(f32[2,3,1024,256]{3,0,1,2:T(2,128)} %copy.142), calls=%async_computation.1 | async-start | bytes 12582912 | tf_op jit(solution)/shard_map/all_to_all | solution.py:60
  215.6 4.1 copy-start.4
  222.1 4.0 copy-start.9
  222.1 4.0 copy-start.10
  226.1 5.6 copy-start.7
  226.1 7.3 copy-start.8
  292.4 42.3 %all-to-all-start.2 = ((f32[2,3,8,128,128]{4,3,1,0,2:T(8,128)}), f32[2,3,8,128,128]{4,3,1,0,2:T(8,128)}, u32[]{:S(2)}, u32[]{:S(2)}) async-start(f32[2,3,8,128,128]{4,3,1,0,2:T(8,128)} %copy.148), calls=%async_computation.2 | async-start | bytes 6291456 | tf_op jit(solution)/shard_map/all_to_all | solution.py:84
  334.7 41.5 %all-to-all-start.3 = ((f32[2,3,8,128,128]{4,3,1,0,2:T(8,128)}), f32[2,3,8,128,128]{4,3,1,0,2:T(8,128)S(1)}, u32[]{:S(2)}, u32[]{:S(2)}) async-start(f32[2,3,8,128,128]{4,3,1,0,2:T(8,128)} %copy.150), calls=%async_computation.3 | async-start | bytes 6291456 | tf_op jit(solution)/shard_map/all_to_all | solution.py:85
  338.4 118.4 %reduce-scatter.2.cloned.1.call-start = ((), (), s32[]{:S(2)}) async-start(), calls=%async_computation.9 | async-start | bytes 655360 | tf_op jit(solution)/shard_map/reduce_scatter | solution.py:151
  379.7 4.7 copy-start.12
  428.4 4.6 copy-start
  428.4 4.6 copy-start.16
  533.1 42.3 %all-to-all-start.4 = ((f32[2,3,128,8,128]{4,2,1,0,3:T(8,128)}), f32[2,3,128,8,128]{4,2,1,0,3:T(8,128)}, u32[]{:S(2)}, u32[]{:S(2)}) async-start(f32[2,3,128,8,128]{4,2,1,0,3:T(8,128)} %copy.152), calls=%async_computation.5 | async-start | bytes 6291456 | tf_op jit(solution)/shard_map/all_to_all | solution.py:98
  575.5 41.5 %all-to-all-start.5 = ((f32[2,3,128,8,128]{4,2,1,0,3:T(8,128)}), f32[2,3,128,8,128]{4,2,1,0,3:T(8,128)S(1)}, u32[]{:S(2)}, u32[]{:S(2)}) async-start(f32[2,3,128,8,128]{4,2,1,0,3:T(8,128)} %copy.154), calls=%async_computation.6 | async-start | bytes 6291456 | tf_op jit(solution)/shard_map/all_to_all | solution.py:99
  619.4 4.7 copy-start.11
  624.1 43.7 %copy-start.13 = (f32[128,1024]{1,0:T(8,128)S(1)}, f32[128,1024]{1,0:T(8,128)}, u32[]{:S(2)}) copy-start(f32[128,1024]{1,0:T(8,128)} %param.10) | copy-start | bytes 1572868
  624.1 43.7 %copy-start.14 = (f32[128,1024]{1,0:T(8,128)S(1)}, f32[128,1024]{1,0:T(8,128)}, u32[]{:S(2)}) copy-start(f32[128,1024]{1,0:T(8,128)} %param.9) | copy-start | bytes 1572868
  686.5 76.4 %all-to-all-start.7 = ((f32[2,3,128,2048]{2,0,1,3:T(2,128)}), f32[2,3,128,2048]{2,0,1,3:T(2,128)}, u32[]{:S(2)}, u32[]{:S(2)}) async-start(f32[2,3,128,2048]{2,0,1,3:T(2,128)} %pad_maximum_fusion.1), calls=%async_computation.8 | async-start | bytes 12582912 | tf_op jit(solution)/shard_map/all_to_all | solution.py:128
  762.8 76.4 %all-to-all-start.6 = ((f32[2,3,128,2048]{2,0,1,3:T(2,128)}), f32[2,3,128,2048]{2,0,1,3:T(2,128)}, u32[]{:S(2)}, u32[]{:S(2)}) async-start(f32[2,3,128,2048]{2,0,1,3:T(2,128)} %pad_maximum_fusion), calls=%async_computation.7 | async-start | bytes 12582912 | tf_op jit(solution)/shard_map/all_to_all | solution.py:127
  848.3 7.3 copy-start.2
  (2 other events, 3.9 us)
Sparse Core Ops, SparseCore 0:
  434.9 21.8 reduce-scatter.1
where the time goes:
time: 912 us; the launch traced here: 903 us
  waiting for transfers between devices  296 us (32%)
  local copies, waits for them, and re-layouts  263 us (29%)
  matrix products  191 us (21%)
  other arithmetic  77.1 us (8%)
  starting transfers between devices  35.9 us (4%)
  between operations  25.5 us (3%)
  blocking collectives  15.8 us (2%)
    dot_general x4, matrix products, transform(): jnp.einsum(form, jnp.stack([real_part, imag_part]), table, precision=HIGH...  190 us
    all_to_all x1, waiting for transfers between devices, spectral_updates(): lax.all_to_all(placed_imag, 'rows', split_axis=3, concat_axis=2, tiled=True)  58.1 us
    all_to_all x1, waiting for transfers between devices, forward_fields(): lax.all_to_all(jnp.swapaxes(crop_real, 2, 3), 'rows', split_axis=2, conca...  53.4 us
    dynamic_update_slice x6, local copies, waits for them, and re-layouts, add_window(): lax.dynamic_update_slice_in_dim(target, current + jnp.swapaxes(incoming,...  52 us
    all_to_all x1, waiting for transfers between devices, forward_fields(): lax.all_to_all(half_real.reshape(blocked), 'rows', split_axis=2, concat_a...  36 us
    all_to_all x1, waiting for transfers between devices, spectral_updates(): lax.all_to_all(col_real.reshape(blocked), 'rows', split_axis=3, concat_ax...  34.9 us
    all_to_all x1, waiting for transfers between devices, spectral_updates(): lax.all_to_all(col_imag.reshape(blocked), 'rows', split_axis=3, concat_ax...  29.7 us
    all_to_all x1, waiting for transfers between devices, forward_fields(): lax.all_to_all(half_imag.reshape(blocked), 'rows', split_axis=2, concat_a...  27.8 us
  transfers between devices with their start and end apart: 9, of which 9 were waited for; matrix products, arithmetic and copies ran while one was open for 18% of the time, Pallas kernels for 0%

commit v1 on v0

--- a/solution.py
+++ b/solution.py
@@ -1,8 +1,13 @@
+import functools
 import math
 
 import jax
 import jax.numpy as jnp
+import ml_dtypes
+import numpy as np
 from jax import lax
+from jax.experimental import pallas as pl
+from jax.experimental.pallas import tpu as pltpu
 from jax.sharding import PartitionSpec as P
 
 FLOOR_TERM = 0.5
@@ -168,6 +173,366 @@
     return (spec_real, spec_imag)
 
 
+RADIX = 4
+VMEM_LIMIT = 56 * 1024 * 1024
+
+
+def split_pair(table):
+    high = table.astype(ml_dtypes.bfloat16)
+    low = (table - high.astype(np.float64)).astype(ml_dtypes.bfloat16)
+    return np.stack([high, low])
+
+
+def radix_tables(length):
+    part = length // RADIX
+    t = np.arange(RADIX)[:, None, None]
+    r = np.arange(part)[None, :, None]
+    s = np.arange(part)[None, None, :]
+    angles = (r * (t + RADIX * s) % length) * (2.0 * np.pi / length)
+    cos_t = np.cos(angles) / np.sqrt(length)
+    sin_t = np.sin(angles) / np.sqrt(length)
+    swap = lambda x: np.swapaxes(x, 1, 2)
+    return (
+        split_pair(np.concatenate([cos_t, sin_t], axis=2)),
+        split_pair(np.concatenate([swap(cos_t), swap(sin_t)], axis=1)),
+        split_pair(np.concatenate([cos_t, sin_t], axis=1)),
+        split_pair(np.concatenate([swap(cos_t), swap(sin_t)], axis=2)),
+    )
+
+
+def halves(x):
+    high = x.astype(jnp.bfloat16)
+    low = (x - high.astype(jnp.float32)).astype(jnp.bfloat16)
+    return high, low
+
+
+def dot(a, b):
+    return jnp.dot(a, b, preferred_element_type=jnp.float32)
+
+
+def dot_right(x, table_ref, t):
+    high, low = halves(x)
+    return dot(high, table_ref[0, t]) + dot(low, table_ref[0, t]) + dot(high, table_ref[1, t])
+
+
+def dot_left(table_ref, t, x):
+    high, low = halves(x)
+    return dot(table_ref[0, t], high) + dot(table_ref[0, t], low) + dot(table_ref[1, t], high)
+
+
+def butterfly(reals, imags, sign):
+    sum_r, sum_i = reals[0] + reals[2], imags[0] + imags[2]
+    dif_r, dif_i = reals[0] - reals[2], imags[0] - imags[2]
+    odd_r, odd_i = reals[1] + reals[3], imags[1] + imags[3]
+    rot_r = sign * (imags[3] - imags[1])
+    rot_i = sign * (reals[1] - reals[3])
+    return (
+        [sum_r + odd_r, dif_r + rot_r, sum_r - odd_r, dif_r - rot_r],
+        [sum_i + odd_i, dif_i + rot_i, sum_i - odd_i, dif_i - rot_i],
+    )
+
+
+def lit_offsets(mask_ref, offsets_ref, nth):
+    row, col, seen = jnp.int32(0), jnp.int32(0), jnp.int32(0)
+    for led in range(offsets_ref.shape[0]):
+        lit = mask_ref[0, led] != 0
+        take = jnp.logical_and(lit, seen == nth)
+        row = jnp.where(take, offsets_ref[led, 0], row)
+        col = jnp.where(take, offsets_ref[led, 1], col)
+        seen = seen + lit.astype(jnp.int32)
+    return row, col
+
+
+def pupil_send_kernel(nth, mask_ref, offsets_ref, real_ref, imag_ref, out_ref):
+    row, _ = lit_offsets(mask_ref, offsets_ref, nth)
+    length = real_ref.shape[1]
+    part = length // RADIX
+    for index, ref in enumerate((real_ref, imag_ref)):
+        rolled = pltpu.roll(ref[...], lax.rem(row, length), 1)
+        for q in range(RADIX):
+            block = rolled[:, q * part : (q + 1) * part].T
+            out_ref[q, index] = block
+            out_ref[q + RADIX, index] = block
+
+
+def window_pupil(nth, mask_ref, offsets_ref, place_ref, pupil_ref, row_base):
+    row, col = lit_offsets(mask_ref, offsets_ref, nth)
+    blocks, _, rows, width = pupil_ref.shape
+    length = blocks * width
+    upper, first = place_ref[0], place_ref[1]
+    position = first + row_base + lax.broadcasted_iota(jnp.int32, (rows, length), 0)
+    owned = (position < row).astype(jnp.int32) == upper
+    parts = []
+    for index in range(2):
+        whole = jnp.concatenate([pupil_ref[d, index] for d in range(blocks)], axis=1)
+        whole = pltpu.roll(whole, lax.rem(col, length), 1)
+        parts.append(jnp.where(owned, whole, 0.0))
+    wrapped = lax.broadcasted_iota(jnp.int32, (rows, length), 1) < col
+    return parts[0], parts[1], wrapped
+
+
+def columns_kernel(
+    nth, mask_ref, offsets_ref, place_ref, real_ref, imag_ref, pupil_ref, table_ref, out_ref
+):
+    rows, size_k = real_ref.shape[1:]
+    length = size_k // 2
+    part = length // RADIX
+    base = pl.program_id(0) * rows
+    p_r, p_i, wrapped = window_pupil(nth, mask_ref, offsets_ref, place_ref, pupil_ref, base)
+    w_r = jnp.where(wrapped, real_ref[0, :, length:], real_ref[0, :, :length])
+    w_i = jnp.where(wrapped, imag_ref[0, :, length:], imag_ref[0, :, :length])
+    x_r = p_r * w_r - p_i * w_i
+    x_i = p_r * w_i + p_i * w_r
+    cut = lambda x: [x[:, q * part : (q + 1) * part] for q in range(RADIX)]
+    y_r, y_i = butterfly(cut(x_r), cut(x_i), 1.0)
+    half = part // 2
+    for t in range(RADIX):
+        both = dot_right(jnp.concatenate([y_r[t], y_i[t]], axis=0), table_ref, t)
+        z_r = both[:rows, :part] - both[rows:, part:]
+        z_i = both[:rows, part:] + both[rows:, :part]
+        for side in range(2):
+            out_ref[2 * t + side, 0] = z_r[:, side * half : (side + 1) * half]
+            out_ref[2 * t + side, 1] = z_i[:, side * half : (side + 1) * half]
+
+
+def rows_kernel(has_total, *refs):
+    if has_total:
+        got_ref, table_ref, before_ref, field_ref, total_ref = refs
+    else:
+        got_ref, table_ref, field_ref, total_ref = refs
+    width = got_ref.shape[3]
+    x_r = [got_ref[q, 0] + got_ref[q + RADIX, 0] for q in range(RADIX)]
+    x_i = [got_ref[q, 1] + got_ref[q + RADIX, 1] for q in range(RADIX)]
+    y_r, y_i = butterfly(x_r, x_i, 1.0)
+    for t in range(RADIX):
+        both = dot_left(table_ref, t, jnp.concatenate([y_r[t], y_i[t]], axis=1))
+        part = both.shape[0] // 2
+        z_r = both[:part, :width] - both[part:, width:]
+        z_i = both[:part, width:] + both[part:, :width]
+        field_ref[0, t] = z_r
+        field_ref[1, t] = z_i
+        power = z_r * z_r + z_i * z_i
+        total_ref[t] = before_ref[t] + power if has_total else power
+
+
+def rows_back_kernel(field_ref, factor_ref, table_ref, out_ref):
+    width = field_ref.shape[3]
+    u_r, u_i = [], []
+    for t in range(RADIX):
+        factor = factor_ref[t]
+        diff = jnp.concatenate([field_ref[0, t] * factor, field_ref[1, t] * factor], axis=1)
+        both = dot_left(table_ref, t, diff)
+        part = both.shape[0] // 2
+        u_r.append(both[:part, :width] + both[part:, width:])
+        u_i.append(both[:part, width:] - both[part:, :width])
+    x_r, x_i = butterfly(u_r, u_i, -1.0)
+    for q in range(RADIX):
+        for side in range(2):
+            out_ref[q + side * RADIX, 0] = x_r[q]
+            out_ref[q + side * RADIX, 1] = x_i[q]
+
+
+def columns_back_kernel(
+    nth, mask_ref, offsets_ref, place_ref, real_ref, imag_ref, pupil_ref, got_ref, table_ref, *outs
+):
+    out_r, out_i = outs[-2:]
+    rows, size_k = real_ref.shape[1:]
+    length = size_k // 2
+    base = pl.program_id(0) * rows
+    p_r, p_i, wrapped = window_pupil(nth, mask_ref, offsets_ref, place_ref, pupil_ref, base)
+    u_r, u_i = [], []
+    for t in range(RADIX):
+        z_r = jnp.concatenate([got_ref[2 * t, 0], got_ref[2 * t + 1, 0]], axis=1)
+        z_i = jnp.concatenate([got_ref[2 * t, 1], got_ref[2 * t + 1, 1]], axis=1)
+        both = dot_right(jnp.concatenate([z_r, z_i], axis=0), table_ref, t)
+        part = both.shape[1] // 2
+        u_r.append(both[:rows, :part] + both[rows:, part:])
+        u_i.append(both[rows:, :part] - both[:rows, part:])
+    x_r, x_i = butterfly(u_r, u_i, -1.0)
+    x_r, x_i = jnp.concatenate(x_r, axis=1), jnp.concatenate(x_i, axis=1)
+    d_r = p_r * x_r + p_i * x_i
+    d_i = p_r * x_i - p_i * x_r
+    for ref, out, delta in ((real_ref, out_r, d_r), (imag_ref, out_i, d_i)):
+        out[0, :, :length] = ref[0, :, :length] + jnp.where(wrapped, 0.0, delta)
+        out[0, :, length:] = ref[0, :, length:] + jnp.where(wrapped, delta, 0.0)
+
+
+SMEM_SPEC = pl.BlockSpec(memory_space=pltpu.SMEM)
+PARAMS = pltpu.CompilerParams(vmem_limit_bytes=VMEM_LIMIT)
+
+
+def fixed(shape):
+    zeros = (0,) * len(shape)
+    return pl.BlockSpec(shape, lambda *_: zeros)
+
+
+def cost(macs, *arrays):
+    moved = sum(math.prod(a.shape) * a.dtype.itemsize for a in arrays)
+    return pl.CostEstimate(flops=2 * macs, bytes_accessed=moved, transcendentals=0)
+
+
+def shaped(shape):
+    return jax.ShapeDtypeStruct(shape, jnp.float32)
+
+
+def exchange(blocks):
+    return lax.all_to_all(blocks, "rows", split_axis=0, concat_axis=0, tiled=True)
+
+
+def fast_body(object_real, object_imag, pupil_real, pupil_imag, measured, source_mask, offsets):
+    width, length = pupil_real.shape
+    modes, local_rows, size_k = object_real.shape
+    groups = lax.axis_size("rows")
+    part = length // RADIX
+    leds = offsets.shape[0]
+    tables = [jnp.asarray(table) for table in radix_tables(length)]
+    place = lax.axis_index("rows")
+    position = jnp.stack([place // RADIX, place % RADIX * local_rows]).astype(jnp.int32)
+    tile = local_rows // 2
+    block_shape = (groups, 2, local_rows, width)
+    dft_macs = 3 * RADIX * 4 * part * part
+    scalars = [SMEM_SPEC] * 3
+    rows_of_mode = lambda mode: pl.BlockSpec((1, tile, size_k), lambda i: (mode, i, 0))
+    tall = pl.BlockSpec((groups, 2, tile, width), lambda i: (0, 0, i, 0))
+
+    def pupil_for(nth):
+        out = shaped(block_shape)
+        return exchange(
+            pl.pallas_call(
+                functools.partial(pupil_send_kernel, nth),
+                out_shape=out,
+                in_specs=[SMEM_SPEC] * 2 + [fixed(pupil_real.shape)] * 2,
+                out_specs=fixed(block_shape),
+                compiler_params=PARAMS,
+                cost_estimate=cost(0, out, pupil_real, pupil_imag),
+                name="pupil_send",
+            )(source_mask, offsets, pupil_real, pupil_imag)
+        )
+
+    def columns(nth, mode, pupil):
+        out = shaped(block_shape)
+        return exchange(
+            pl.pallas_call(
+                functools.partial(columns_kernel, nth),
+                out_shape=out,
+                grid=(local_rows // tile,),
+                in_specs=scalars + [rows_of_mode(mode)] * 2 + [tall, fixed(tables[0].shape)],
+                out_specs=tall,
+                compiler_params=PARAMS,
+                cost_estimate=cost(local_rows * dft_macs, out, out, out, out),
+                name="columns",
+            )(source_mask, offsets, position, object_real, object_imag, pupil, tables[0])
+        )
+
+    def rows(got, total):
+        field = shaped((2, RADIX, part, width))
+        power = shaped((RADIX, part, width))
+        before = [] if total is None else [total]
+        return pl.pallas_call(
+            functools.partial(rows_kernel, bool(before)),
+            out_shape=(field, power),
+            in_specs=[fixed(got.shape), fixed(tables[1].shape)] + [fixed(b.shape) for b in before],
+            out_specs=(fixed(field.shape), fixed(power.shape)),
+            compiler_params=PARAMS,
+            cost_estimate=cost(width * dft_macs, got, field, power),
+            name="rows",
+        )(got, tables[1], *before)
+
+    def rows_back(field, factor):
+        out = shaped(block_shape)
+        return exchange(
+            pl.pallas_call(
+                rows_back_kernel,
+                out_shape=out,
+                in_specs=[fixed(field.shape), fixed(factor.shape), fixed(tables[2].shape)],
+                out_specs=fixed(block_shape),
+                compiler_params=PARAMS,
+                cost_estimate=cost(width * dft_macs, out, field, factor),
+                name="rows_back",
+            )(field, factor, tables[2])
+        )
+
+    def columns_back(nth, mode, pupil, got, current, written):
+        operands = [source_mask, offsets, position, *current, pupil, got, tables[3]]
+        specs = scalars + [rows_of_mode(mode)] * 2 + [tall, tall, fixed(tables[3].shape)]
+        if written is None:
+            aliases = {}
+        elif written is current:
+            aliases = {3: 0, 4: 1}
+        else:
+            aliases = {len(operands): 0, len(operands) + 1: 1}
+            operands += written
+            specs += [pl.BlockSpec(memory_space=pl.ANY)] * 2
+        out = shaped(object_real.shape)
+        return pl.pallas_call(
+            functools.partial(columns_back_kernel, nth),
+            out_shape=(out, out),
+            grid=(local_rows // tile,),
+            in_specs=specs,
+            out_specs=(rows_of_mode(mode), rows_of_mode(mode)),
+            input_output_aliases=aliases,
+            compiler_params=PARAMS,
+            cost_estimate=cost(local_rows * dft_macs, got, got, got, got),
+            name="columns_back",
+        )(*operands)
+
+    def measured_share():
+        level = lax.axis_index("mode")
+        mine = lax.dynamic_index_in_dim(
+            measured[0].reshape(width // RADIX, RADIX, length), level, 1, keepdims=False
+        )
+        sent = jnp.transpose(mine.reshape(width // RADIX, part, RADIX), (2, 1, 0))
+        sent = jnp.swapaxes(sent.reshape(groups, width, width // RADIX), 1, 2)
+        return exchange(sent).reshape(1, part, width)
+
+    def update(count):
+        def run(*_):
+            pupils = [pupil_for(nth) for nth in range(count)]
+            got = {}
+            for nth in range(count):
+                for mode in range(modes):
+                    got[nth, mode] = columns(nth, mode, pupils[nth])
+            amplitude = measured_share()
+            total, fields = None, {}
+            for key, blocks in got.items():
+                fields[key], total = rows(blocks, total)
+            share = lax.psum_scatter(total, "mode", scatter_dimension=0, tiled=True)
+            ratio = amplitude / jnp.sqrt(share + FLOOR_TERM) - 1.0
+            factor = lax.all_gather(ratio, "mode", axis=0, tiled=True)
+            back = {key: rows_back(field, factor) for key, field in fields.items()}
+            current, written = (object_real, object_imag), None
+            for nth in range(count):
+                for mode in range(modes):
+                    written = columns_back(
+                        nth, mode, pupils[nth], back[nth, mode], current, written
+                    )
+                    if nth > 0:
+                        current = written
+                current = written
+            return tuple(written)
+
+        return run
+
+    lit = jnp.sum((source_mask[0] != 0).astype(jnp.int32))
+    most = max(leds - 1, 1)
+    if most == 1:
+        return update(1)()
+    return lax.switch(jnp.clip(lit - 1, 0, most - 1), [update(n + 1) for n in range(most)])
+
+
+def fits_fast(mesh, object_shape, pupil_shape):
+    groups, levels = mesh.shape["rows"], mesh.shape["mode"]
+    length, size_k = pupil_shape[1], object_shape[2]
+    local_rows = size_k // groups
+    return (
+        size_k == 2 * length
+        and groups == 2 * RADIX
+        and levels == RADIX
+        and local_rows % 256 == 0
+        and (length // groups) % 128 == 0
+    )
+
+
 def solution(mesh):
     in_specs = (
         P("mode", "rows", None),
@@ -179,4 +544,16 @@
         P(),
     )
     out_specs = (P("mode", "rows", None), P("mode", "rows", None))
-    return jax.shard_map(body, mesh=mesh, in_specs=in_specs, out_specs=out_specs, check_vma=False)
+
+    def chosen(object_real, object_imag, pupil_real, *others):
+        fast = fits_fast(mesh, object_real.shape, pupil_real.shape)
+        mapped = jax.shard_map(
+            fast_body if fast else body,
+            mesh=mesh,
+            in_specs=in_specs,
+            out_specs=out_specs,
+            check_vma=False,
+        )
+        return mapped(object_real, object_imag, pupil_real, *others)
+
+    return chosen

time: 912 us -> 237 us (0.26)
  local copies, waits for them, and re-layouts: 263 us -> 2.16 us
  waiting for transfers between devices: 296 us -> 99.2 us
  matrix products: 191 us -> 0 us
  other arithmetic: 77.1 us -> 2.3 us
  Pallas kernels: 0 us -> 43.2 us
  blocking collectives: 15.8 us -> 56.6 us
  starting transfers between devices: 35.9 us -> 17.6 us
  between operations: 25.5 us -> 14.7 us
    dot_general x5 -> x0, matrix products: 191 us -> none  [the longest x4 190 us: transform(): jnp.einsum(form, jnp.stack([real_part, imag_part]), table, precision=HIGH...]
    all_to_all x8 -> x4, waiting for transfers between devices: 274 us -> 86.3 us  [exchange(): lax.all_to_all(blocks, 'rows', split_axis=0, concat_axis=0, tiled=True)]
    all_to_all x13 -> x0, local copies, waits for them, and re-layouts: 75.4 us -> none  [the longest x3 19 us: spectral_updates(): lax.all_to_all(placed_imag, 'rows', split_axis=3, concat_axis=2, tiled=True)]
    dynamic_update_slice x12 -> x0, local copies, waits for them, and re-layouts: 54.1 us -> none  [the longest x6 52 us: add_window(): lax.dynamic_update_slice_in_dim(target, current + jnp.swapaxes(incoming,...]
    pallas_call x0 -> x9, Pallas kernels: none -> 43.2 us  [the longest x2 12.9 us: columns_back(): pl.pallas_call(functools.partial(columns_back_kernel, nth), out_shape=(ou...]
    all_to_all x0 -> x2, blocking collectives: none -> 40.1 us  [exchange(): lax.all_to_all(blocks, 'rows', split_axis=0, concat_axis=0, tiled=True)]
    dynamic_slice x13 -> x1, local copies, waits for them, and re-layouts: 34.4 us -> 0.14 us  [measured_share(): lax.dynamic_index_in_dim(measured[0].reshape(width // RADIX, RADIX, lengt...]
    slice x12 -> x0, local copies, waits for them, and re-layouts: 27.1 us -> none  [the longest x4 8.53 us: spectral_updates(): upd_imag[:, source_index]]
  transfers between devices with their start and end apart: 9 -> 5, of which waited for: 9 -> 5; matrix products, arithmetic and copies ran while one was open for 18% -> 0% of each run, Pallas kernels for 0% -> 8%
where the time goes in v1:
time: 237 us; the launch traced here: 236 us
  waiting for transfers between devices  99.2 us (42%)
  blocking collectives  56.6 us (24%)
  Pallas kernels  43.2 us (18%)
  starting transfers between devices  17.6 us (7%)
  between operations  14.7 us (6%)
    all_to_all x4, waiting for transfers between devices, exchange(): lax.all_to_all(blocks, 'rows', split_axis=0, concat_axis=0, tiled=True)  86.3 us
    all_to_all x2, blocking collectives, exchange(): lax.all_to_all(blocks, 'rows', split_axis=0, concat_axis=0, tiled=True)  40.1 us
    all_to_all x4, starting transfers between devices, exchange(): lax.all_to_all(blocks, 'rows', split_axis=0, concat_axis=0, tiled=True)  17.6 us
    all_gather x1, blocking collectives, run(): factor = lax.all_gather(ratio, 'mode', axis=0, tiled=True)  16.6 us
    pallas_call x2, Pallas kernels, columns_back(): pl.pallas_call(functools.partial(columns_back_kernel, nth), out_shape=(ou...  12.9 us
    reduce_scatter x1, waiting for transfers between devices, run(): share = lax.psum_scatter(total, 'mode', scatter_dimension=0, tiled=True)  12.9 us
    pallas_call x2, Pallas kernels, columns(): pl.pallas_call(functools.partial(columns_kernel, nth), out_shape=out, gri...  11.3 us
    pallas_call x2, Pallas kernels, rows(): pl.pallas_call(functools.partial(rows_kernel, bool(before)), out_shape=(f...  7.84 us
  transfers between devices with their start and end apart: 5, of which 5 were waited for; matrix products, arithmetic and copies ran while one was open for 0% of the time, Pallas kernels for 8%

profile of v1, /device:TPU:0, one launch (start us, length us, event | category | flops | bytes accessed | tf_op | source)
XLA Modules:
  0.0 236.0 jit_solution(13304301489103485476)
XLA Ops:
  7.3 1.3 fusion.2
  9.2 219.9 %conditional.1 = ((f32[2,256,2048]{2,1,0:T(8,128)}, f32[2,256,2048]{2,1,0:T(8,128)})) conditional(s32[]{:T(128)} %clamp.3, (s32[1,3]{1,0:T(1,128)}, s32[3,2]{0,1:T(2,128)}, f32[128,1024]{1,0:T(8,128)}, f32[128,1024]{1,0:T(8,128)}, s32[2]{0:T(128)S(1)}, /*index=5*/f32[2,256,2048]{2,1,0:T(8,128)}, f32[2,256,2048]{2,1,0:T(8,128)}, ...), branch_computations={%region_1.3_spmd, %region_3.5_spmd} | conditional | flops 19327451136 | bytes 227934976 | solution.py:520
  9.2 1.3 copy.41.offsets_ref
  10.6 3.4 %pupil_send.3 = f32[8,2,256,128]{3,2,1,0:T(8,128)} custom-call(s32[1,3]{1,0:T(1,128)} %get-tuple-element.48.mask_ref, s32[3,2]{1,0:T(4,128)} %copy.41.offsets_ref, f32[128,1024]{1,0:T(8,128)} %get-tuple-element.53.real_ref, f32[128,1024]{1,0:T(8,128)} %get-tuple-element.54.imag_ref), custom_call_target="tpu_custom_call" | custom-call | bytes 3145728 | tf_op jit(solution)/shard_map/cond/branch_0_fun/pupil_send/pallas_call | solution.py:401
  13.9 32.1 %all_to_all.68.pupil_ref = f32[8,2,256,128]{3,2,1,0:T(8,128)} all-to-all(f32[8,2,256,128]{3,2,1,0:T(8,128)} %pupil_send.3), channel_id=1, replica_groups=mesh['mode'=4,'rows'=8] {'rows'}, dimensions={0} | all-to-all | bytes 4194304 | tf_op jit(solution)/shard_map/cond/branch_0_fun/all_to_all | solution.py:379
  46.1 5.5 %columns.7 = f32[8,2,256,128]{3,2,1,0:T(8,128)} custom-call(s32[1,3]{1,0:T(1,128)S(1)} %copy-done.14, s32[3,2]{1,0:T(4,128)} %copy.41.offsets_ref, s32[2]{0:T(128)S(1)} %get-tuple-element.50.place_ref, f32[2,256,2048]{2,1,0:T(8,128)S(1)} %copy-done, f32[2,256,2048]{2,1,0:T(8,128)} %get-tuple-element.52.imag_ref, f32[8,2,256,128]{3,2,1,0:T(8,128)} %all_to_all.68.pupil_ref, ...), custom_call_target="tpu_custom_call" | custom-call | flops 1610612736 | bytes 8388608 | tf_op jit(solution)/shard_map/cond/branch_0_fun/columns/pallas_call | solution.py:415
  51.6 4.4 %all-to-all-start.2 = ((f32[8,2,256,128]{3,2,1,0:T(8,128)}), f32[8,2,256,128]{3,2,1,0:T(8,128)}, u32[]{:S(2)}, u32[]{:S(2)}) async-start(f32[8,2,256,128]{3,2,1,0:T(8,128)} %columns.7), calls=%async_computation.2 | async-start | bytes 4194304 | tf_op jit(solution)/shard_map/cond/branch_0_fun/all_to_all | solution.py:379
  55.9 5.8 %columns.6 = f32[8,2,256,128]{3,2,1,0:T(8,128)} custom-call(s32[1,3]{1,0:T(1,128)S(1)} %copy-done.14, s32[3,2]{1,0:T(4,128)} %copy.41.offsets_ref, s32[2]{0:T(128)S(1)} %get-tuple-element.50.place_ref, f32[2,256,2048]{2,1,0:T(8,128)} %get-tuple-element.51.real_ref, f32[2,256,2048]{2,1,0:T(8,128)} %get-tuple-element.52.imag_ref, ...), custom_call_target="tpu_custom_call" | custom-call | flops 1610612736 | bytes 8388608 | tf_op jit(solution)/shard_map/cond/branch_0_fun/columns/pallas_call | solution.py:415
  61.7 20.8 %all-to-all-done.2.refs_0_ = f32[8,2,256,128]{3,2,1,0:T(8,128)} async-done(((f32[8,2,256,128]{3,2,1,0:T(8,128)}), f32[8,2,256,128]{3,2,1,0:T(8,128)}, u32[]{:S(2)}, u32[]{:S(2)}) %all-to-all-start.2) | async-done | bytes 2097184 | tf_op jit(solution)/shard_map/cond/branch_0_fun/all_to_all | solution.py:379
  82.6 4.3 %all-to-all-start.1 = ((f32[8,2,256,128]{3,2,1,0:T(8,128)}), f32[8,2,256,128]{3,2,1,0:T(8,128)}, u32[]{:S(2)}, u32[]{:S(2)}) async-start(f32[8,2,256,128]{3,2,1,0:T(8,128)} %columns.6), calls=%async_computation.1 | async-start | bytes 4194304 | tf_op jit(solution)/shard_map/cond/branch_0_fun/all_to_all | solution.py:379
  87.0 3.9 %rows.6 = (f32[2,4,256,128]{3,2,1,0:T(8,128)}, f32[4,256,128]{2,1,0:T(8,128)}) custom-call(f32[8,2,256,128]{3,2,1,0:T(8,128)} %all-to-all-done.2.refs_0_, bf16[2,4,512,256]{3,2,1,0:T(8,128)(2,1)S(1)} %copy-done.2), custom_call_target="tpu_custom_call" | custom-call | flops 805306368 | bytes 3670016 | tf_op jit(solution)/shard_map/cond/branch_0_fun/rows/pallas_call | solution.py:431
  90.8 22.7 %all-to-all-done.1.refs_0_ = f32[8,2,256,128]{3,2,1,0:T(8,128)} async-done(((f32[8,2,256,128]{3,2,1,0:T(8,128)}), f32[8,2,256,128]{3,2,1,0:T(8,128)}, u32[]{:S(2)}, u32[]{:S(2)}) %all-to-all-start.1) | async-done | bytes 2097184 | tf_op jit(solution)/shard_map/cond/branch_0_fun/all_to_all | solution.py:379
  113.6 4.0 %rows.7 = (f32[2,4,256,128]{3,2,1,0:T(8,128)}, f32[4,256,128]{2,1,0:T(8,128)}) custom-call(f32[8,2,256,128]{3,2,1,0:T(8,128)} %all-to-all-done.1.refs_0_, bf16[2,4,512,256]{3,2,1,0:T(8,128)(2,1)S(1)} %copy-done.2, f32[4,256,128]{2,1,0:T(8,128)} %get-tuple-element.57.refs_2_), custom_call_target="tpu_custom_call" | custom-call | flops 805306368 | bytes 3670016 | tf_op jit(solution)/shard_map/cond/branch_0_fun/rows/pallas_call | solution.py:431
  118.4 7.9 %all_to_all.69 = f32[8,32,128]{2,1,0:T(8,128)S(1)} all-to-all(f32[8,32,128]{2,1,0:T(8,128)S(1)} %copy.37), channel_id=1, replica_groups=mesh['mode'=4,'rows'=8] {'rows'}, dimensions={0} | all-to-all | bytes 262144 | tf_op jit(solution)/shard_map/cond/branch_0_fun/all_to_all | solution.py:379
  126.4 12.9 %reduce-scatter.3.cloned.1.call-done = f32[1,256,128]{2,1,0:T(8,128)} async-done(((f32[4,256,128]{2,1,0:T(8,128)}), f32[1,256,128]{2,1,0:T(8,128)}) %reduce-scatter.3.cloned.1.call-update) | async-done | bytes 131088 | tf_op jit(solution)/shard_map/cond/branch_0_fun/reduce_scatter | solution.py:499
  140.2 16.6 %all_gather.4.factor_ref = f32[4,256,128]{2,1,0:T(8,128)} all-gather(f32[1,256,128]{2,1,0:T(8,128)S(1)} %fusion), channel_id=1, replica_groups=mesh['mode'=4,'rows'=8] {'mode'}, dimensions={0}, use_global_device_ids=true | all-gather | bytes 655360 | tf_op jit(solution)/shard_map/cond/branch_0_fun/all_gather | solution.py:501
  156.8 3.8 %rows_back.7 = f32[8,2,256,128]{3,2,1,0:T(8,128)} custom-call(f32[2,4,256,128]{3,2,1,0:T(8,128)} %get-tuple-element.63.field_ref, f32[4,256,128]{2,1,0:T(8,128)} %all_gather.4.factor_ref, bf16[2,4,512,256]{3,2,1,0:T(8,128)(2,1)S(1)} %copy-done.8), custom_call_target="tpu_custom_call" | custom-call | flops 805306368 | bytes 3670016 | tf_op jit(solution)/shard_map/cond/branch_0_fun/rows_back/pallas_call | solution.py:444
  160.6 4.3 %all-to-all-start.5 = ((f32[8,2,256,128]{3,2,1,0:T(8,128)}), f32[8,2,256,128]{3,2,1,0:T(8,128)}, u32[]{:S(2)}, u32[]{:S(2)}) async-start(f32[8,2,256,128]{3,2,1,0:T(8,128)} %rows_back.7), calls=%async_computation.6 | async-start | bytes 4194304 | tf_op jit(solution)/shard_map/cond/branch_0_fun/all_to_all | solution.py:379
  165.0 3.9 %rows_back.6 = f32[8,2,256,128]{3,2,1,0:T(8,128)} custom-call(f32[2,4,256,128]{3,2,1,0:T(8,128)} %get-tuple-element.58.field_ref, f32[4,256,128]{2,1,0:T(8,128)} %all_gather.4.factor_ref, bf16[2,4,512,256]{3,2,1,0:T(8,128)(2,1)S(1)} %copy-done.8), custom_call_target="tpu_custom_call" | custom-call | flops 805306368 | bytes 3670016 | tf_op jit(solution)/shard_map/cond/branch_0_fun/rows_back/pallas_call | solution.py:444
  168.9 22.7 %all-to-all-done.5.got_ref = f32[8,2,256,128]{3,2,1,0:T(8,128)} async-done(((f32[8,2,256,128]{3,2,1,0:T(8,128)}), f32[8,2,256,128]{3,2,1,0:T(8,128)}, u32[]{:S(2)}, u32[]{:S(2)}) %all-to-all-start.5) | async-done | bytes 2097184 | tf_op jit(solution)/shard_map/cond/branch_0_fun/all_to_all | solution.py:379
  191.6 4.5 %all-to-all-start.4 = ((f32[8,2,256,128]{3,2,1,0:T(8,128)}), f32[8,2,256,128]{3,2,1,0:T(8,128)}, u32[]{:S(2)}, u32[]{:S(2)}) async-start(f32[8,2,256,128]{3,2,1,0:T(8,128)} %rows_back.6), calls=%async_computation.5 | async-start | bytes 4194304 | tf_op jit(solution)/shard_map/cond/branch_0_fun/all_to_all | solution.py:379
  196.2 6.5 %columns_back.6 = (f32[2,256,2048]{2,1,0:T(8,128)}, f32[2,256,2048]{2,1,0:T(8,128)}) custom-call(s32[1,3]{1,0:T(1,128)S(1)} %copy-done.14, s32[3,2]{1,0:T(4,128)} %copy.41.offsets_ref, s32[2]{0:T(128)S(1)} %get-tuple-element.50.place_ref, f32[2,256,2048]{2,1,0:T(8,128)} %get-tuple-element.51.real_ref, f32[2,256,2048]{2,1,0:T(8,128)} %get-tuple-element.52.imag_ref, ...), custom_call_target="tpu_custom_call" | custom-call | flops 1610612736 | bytes 8388608 | tf_op jit(solution)/shard_map/cond/branch_0_fun/columns_back/pallas_call | solution.py:467
  202.7 20.0 %all-to-all-done.4.got_ref = f32[8,2,256,128]{3,2,1,0:T(8,128)} async-done(((f32[8,2,256,128]{3,2,1,0:T(8,128)}), f32[8,2,256,128]{3,2,1,0:T(8,128)}, u32[]{:S(2)}, u32[]{:S(2)}) %all-to-all-start.4) | async-done | bytes 2097184 | tf_op jit(solution)/shard_map/cond/branch_0_fun/all_to_all | solution.py:379
  222.7 6.5 %columns_back.7 = (f32[2,256,2048]{2,1,0:T(8,128)}, f32[2,256,2048]{2,1,0:T(8,128)}) custom-call(s32[1,3]{1,0:T(1,128)S(1)} %copy-done.14, s32[3,2]{1,0:T(4,128)} %copy.41.offsets_ref, s32[2]{0:T(128)S(1)} %get-tuple-element.50.place_ref, f32[2,256,2048]{2,1,0:T(8,128)} %get-tuple-element.51.real_ref, ...), custom_call_target="tpu_custom_call", output_to_operand_aliasing={{0}: (8, {}), {1}: (9, {})} | custom-call | flops 1610612736 | bytes 8388608 | tf_op jit(solution)/shard_map/cond/branch_0_fun/columns_back/pallas_call | solution.py:467
  (24 shorter events, 1.9 us)
Async XLA Ops:
  10.6 35.5 %copy-start.6 = (bf16[2,4,256,512]{3,2,1,0:T(8,128)(2,1)S(1)}, bf16[2,4,256,512]{3,2,1,0:T(8,128)(2,1)}, u32[]{:S(2)}) copy-start(bf16[2,4,256,512]{3,2,1,0:T(8,128)(2,1)} %get-tuple-element.55.table_ref) | copy-start | bytes 6291460 | tf_op jit(solution)/shard_map/cond
  13.9 32.1 %copy-start = (f32[2,256,2048]{2,1,0:T(8,128)S(1)}, f32[2,256,2048]{2,1,0:T(8,128)}, u32[]{:S(2)}) copy-start(f32[2,256,2048]{2,1,0:T(8,128)} %get-tuple-element.51.real_ref) | copy-start | bytes 12582916 | tf_op jit(solution)/shard_map/cond
  13.9 32.1 %copy-start.14 = (s32[1,3]{1,0:T(1,128)S(1)}, s32[1,3]{1,0:T(1,128)}, u32[]{:S(2)}) copy-start(s32[1,3]{1,0:T(1,128)} %get-tuple-element.48.mask_ref) | copy-start | bytes 40 | tf_op jit(solution)/shard_map/cond
  51.6 31.0 %all-to-all-start.2 = ((f32[8,2,256,128]{3,2,1,0:T(8,128)}), f32[8,2,256,128]{3,2,1,0:T(8,128)}, u32[]{:S(2)}, u32[]{:S(2)}) async-start(f32[8,2,256,128]{3,2,1,0:T(8,128)} %columns.7), calls=%async_computation.2 | async-start | bytes 4194304 | tf_op jit(solution)/shard_map/cond/branch_0_fun/all_to_all | solution.py:379
  61.7 25.2 %copy-start.2 = (bf16[2,4,512,256]{3,2,1,0:T(8,128)(2,1)S(1)}, bf16[2,4,512,256]{3,2,1,0:T(8,128)(2,1)}, u32[]{:S(2)}) copy-start(bf16[2,4,512,256]{3,2,1,0:T(8,128)(2,1)} %get-tuple-element.56.refs_1_) | copy-start | bytes 6291460 | tf_op jit(solution)/shard_map/cond
  82.6 31.0 %all-to-all-start.1 = ((f32[8,2,256,128]{3,2,1,0:T(8,128)}), f32[8,2,256,128]{3,2,1,0:T(8,128)}, u32[]{:S(2)}, u32[]{:S(2)}) async-start(f32[8,2,256,128]{3,2,1,0:T(8,128)} %columns.6), calls=%async_computation.1 | async-start | bytes 4194304 | tf_op jit(solution)/shard_map/cond/branch_0_fun/all_to_all | solution.py:379
  86.9 52.3 %reduce-scatter.3.cloned.1.call-start = ((), (), s32[]{:S(2)}) async-start(), calls=%async_computation.19 | async-start | bytes 655360 | tf_op jit(solution)/shard_map/cond/branch_0_fun/reduce_scatter | solution.py:499
  113.6 4.0 %copy-start.12 = (f32[1,128,1024]{2,1,0:T(8,128)S(1)}, f32[1,128,1024]{2,1,0:T(8,128)}, u32[]{:S(2)}) copy-start(f32[1,128,1024]{2,1,0:T(8,128)} %get-tuple-element.59) | copy-start | bytes 1572868 | tf_op jit(solution)/shard_map/cond
  117.6 39.2 %copy-start.8 = (bf16[2,4,512,256]{3,2,1,0:T(8,128)(2,1)S(1)}, bf16[2,4,512,256]{3,2,1,0:T(8,128)(2,1)}, u32[]{:S(2)}) copy-start(bf16[2,4,512,256]{3,2,1,0:T(8,128)(2,1)} %get-tuple-element.61.table_ref) | copy-start | bytes 6291460 | tf_op jit(solution)/shard_map/cond
  160.6 31.0 %all-to-all-start.5 = ((f32[8,2,256,128]{3,2,1,0:T(8,128)}), f32[8,2,256,128]{3,2,1,0:T(8,128)}, u32[]{:S(2)}, u32[]{:S(2)}) async-start(f32[8,2,256,128]{3,2,1,0:T(8,128)} %rows_back.7), calls=%async_computation.6 | async-start | bytes 4194304 | tf_op jit(solution)/shard_map/cond/branch_0_fun/all_to_all | solution.py:379
  168.9 27.3 %copy-start.4 = (bf16[2,4,256,512]{3,2,1,0:T(8,128)(2,1)S(1)}, bf16[2,4,256,512]{3,2,1,0:T(8,128)(2,1)}, u32[]{:S(2)}) copy-start(bf16[2,4,256,512]{3,2,1,0:T(8,128)(2,1)} %get-tuple-element.62.table_ref) | copy-start | bytes 6291460 | tf_op jit(solution)/shard_map/cond
  191.6 31.0 %all-to-all-start.4 = ((f32[8,2,256,128]{3,2,1,0:T(8,128)}), f32[8,2,256,128]{3,2,1,0:T(8,128)}, u32[]{:S(2)}, u32[]{:S(2)}) async-start(f32[8,2,256,128]{3,2,1,0:T(8,128)} %rows_back.6), calls=%async_computation.5 | async-start | bytes 4194304 | tf_op jit(solution)/shard_map/cond/branch_0_fun/all_to_all | solution.py:379
Sparse Core Ops, SparseCore 0:
  117.7 21.5 reduce-scatter.2
